TPU v7x, 32 devices: a whole 2x2x4 slice. The times are simulated.
32 devices in a mesh: ctx: 16 (over z, x, core), head: 2 (over y).
Axes of the slice: x: 2, y: 2, z: 4, core: 2. Of those that a mesh axis runs over, the one named last changes fastest.
Arguments:
- query: bfloat16 [4096, 32, 128], P('ctx', 'head'), may hold values from -160 to 160
- key: bfloat16 [4096, 8, 128], P('ctx', 'head'), may hold values from -8 to 8
- value: bfloat16 [4096, 8, 128], P('ctx', 'head'), may hold values from -6 to 6
- d_mixed: bfloat16 [4096, 4096], P('ctx', 'head'), may hold values from -6 to 6
- out_weight: bfloat16 [4096, 4096], P('head'), may hold values from -1 to 1
- block_keys: int32 [32, 20], P('ctx'), may hold values from 0 to 31, as said below
- scope_ids: int32 [4096], P('ctx'), may hold values from 0 to 15
Outputs:
- grad_query: bfloat16 [4096, 32, 128], P('ctx', 'head')
- grad_key: bfloat16 [4096, 8, 128], P('ctx', 'head')
- grad_value: bfloat16 [4096, 8, 128], P('ctx', 'head')
Inputs may be any that keep to these rules, and one draw needn't show every extreme that they name: `block_keys`: row b names 20 distinct key blocks, block b itself among them.
All inputs are finite; a program needn't handle non-finite values.
Results may differ from a plain program's by a relative error of at most 0.0059.
Values may be sent and summed in bfloat16 or wider, within the bound.
A program may use at most 192 MiB of HBM per device.

v0:
```python
import math
import jax
import jax.numpy as jnp
from jax import lax
from jax.sharding import PartitionSpec as P

BLK = 128


def score_pair(q_block, scope_q, k_block, scope_k, scale):
    scores = (
        jnp.einsum("ignd,jgd->gnij", q_block, k_block, preferred_element_type=jnp.float32) * scale
    )
    scope_key = scope_k.astype(jnp.float32)
    visible = (scope_key[None, :] == scope_q[:, None]) | (scope_key[None, :] == 0.0)
    return (scores, visible)


def backward_pair(
    q_block, do_block, lse_here, delta_here, scope_q, k_block, v_block, scope_k, scale
):
    scores, visible = score_pair(q_block, scope_q, k_block, scope_k, scale)
    probs = jnp.where(visible, jnp.exp(scores - lse_here[..., None]), 0.0)
    rounded = probs.astype(jnp.bfloat16)
    grad_v = jnp.einsum("gnij,ignd->jgd", rounded, do_block, preferred_element_type=jnp.float32)
    dprobs = jnp.einsum("ignd,jgd->gnij", do_block, v_block, preferred_element_type=jnp.float32)
    dscores = (probs * (dprobs - delta_here[..., None]) * scale).astype(jnp.bfloat16)
    grad_q = jnp.einsum("gnij,jgd->ignd", dscores, k_block, preferred_element_type=jnp.float32)
    grad_k = jnp.einsum("gnij,ignd->jgd", dscores, q_block, preferred_element_type=jnp.float32)
    return (grad_q, grad_k, grad_v)


def on_device(query, key, value, d_mixed, out_weight, block_keys, scope_ids):
    tokens_here = query.shape[0]
    heads_here = query.shape[1]
    width = query.shape[2]
    kv_here = key.shape[1]
    group = heads_here // kv_here
    blocks = tokens_here // BLK
    scale = 1.0 / math.sqrt(width)
    d_out = lax.dot_general(
        lax.all_gather(d_mixed, "head", axis=1, tiled=True),
        out_weight,
        (((1,), (1,)), ((), ())),
        preferred_element_type=jnp.float32,
    ).astype(jnp.bfloat16)
    q_blocks = query.reshape(blocks, BLK, kv_here, group, width)
    do_blocks = d_out.reshape(blocks, BLK, kv_here, group, width)
    own_scope = scope_ids.reshape(blocks, BLK).astype(jnp.float32)
    all_keys, all_values, all_scope = (
        lax.all_gather(key, "ctx", axis=0, tiled=True),
        lax.all_gather(value, "ctx", axis=0, tiled=True),
        lax.all_gather(scope_ids.astype(jnp.bfloat16), "ctx", axis=0, tiled=True),
    )
    total_blocks = all_keys.shape[0] // BLK
    k_all = all_keys.reshape(total_blocks, BLK, kv_here, width)
    v_all = all_values.reshape(total_blocks, BLK, kv_here, width)
    s_all = all_scope.reshape(total_blocks, BLK)
    slots = block_keys.shape[1]
    grad_k_all = jnp.zeros((total_blocks, BLK, kv_here, width), jnp.float32)
    grad_v_all = jnp.zeros((total_blocks, BLK, kv_here, width), jnp.float32)
    grad_rows = []
    for row in range(blocks):
        listed = block_keys[row]
        k_near = k_all[listed].reshape(slots * BLK, kv_here, width)
        v_near = v_all[listed].reshape(slots * BLK, kv_here, width)
        s_near = s_all[listed].reshape(slots * BLK)
        scores, visible = score_pair(q_blocks[row], own_scope[row], k_near, s_near, scale)
        masked = jnp.where(visible, scores, -1e30)
        high = jnp.max(masked, axis=-1)
        total = jnp.sum(jnp.where(visible, jnp.exp(scores - high[..., None]), 0.0), axis=-1)
        lse_here = high + jnp.log(total)
        probs = jnp.where(visible, jnp.exp(scores - lse_here[..., None]), 0.0)
        attn_out = jnp.einsum(
            "gnij,jgd->ignd", probs, v_near.astype(jnp.float32), precision=lax.Precision.HIGHEST
        )
        delta = jnp.sum(do_blocks[row].astype(jnp.float32) * attn_out, axis=-1)
        delta_here = jnp.transpose(delta, (1, 2, 0))
        grad_q, part_k, part_v = backward_pair(
            q_blocks[row],
            do_blocks[row],
            lse_here,
            delta_here,
            own_scope[row],
            k_near,
            v_near,
            s_near,
            scale,
        )
        grad_rows.append(grad_q)
        grad_k_all = grad_k_all.at[listed].add(part_k.reshape(slots, BLK, kv_here, width))
        grad_v_all = grad_v_all.at[listed].add(part_v.reshape(slots, BLK, kv_here, width))
    combined = jnp.concatenate([grad_k_all, grad_v_all], axis=-1).reshape(
        total_blocks * BLK, kv_here, 2 * width
    )
    home = lax.psum_scatter(combined, "ctx", scatter_dimension=0, tiled=True)
    grad_query = jnp.stack(grad_rows).reshape(tokens_here, heads_here, width).astype(jnp.bfloat16)
    grad_key = home[:, :, :width].astype(jnp.bfloat16)
    grad_value = home[:, :, width:].astype(jnp.bfloat16)
    return (grad_query, grad_key, grad_value)


def solution(mesh):
    in_specs = (
        P("ctx", "head", None),
        P("ctx", "head", None),
        P("ctx", "head", None),
        P("ctx", "head"),
        P("head", None),
        P("ctx", None),
        P("ctx"),
    )
    out_specs = (P("ctx", "head", None), P("ctx", "head", None), P("ctx", "head", None))
    return jax.shard_map(
        on_device, mesh=mesh, in_specs=in_specs, out_specs=out_specs, check_vma=False
    )
```

profile of v0, /device:TPU:0, one launch (start us, length us, event | category | flops | bytes accessed | tf_op | source)
XLA Modules:
  0.0 586.1 jit_solution(16674847419327355169)
XLA Ops:
  11.2 23.1 %all-gather = bf16[16,1,256]{2,1,0:T(2,128)(2,1)S(1)} all-gather(bf16[1,1,256]{2,1,0:T(2,128)(2,1)S(1)} %reshape.254), channel_id=1, replica_groups=mesh['ctx'=16,'head'=2] {'ctx'}, dimensions={0}, use_global_device_ids=true | all-gather | bytes 8704 | tf_op jit(solution)/shard_map/all_gather | solution.py:53
  45.4 10.9 %convolution_convert_fusion = bf16[256,2048]{1,0:T(8,128)(2,1)S(1)} fusion(bf16[256,4096]{1,0:T(8,128)(2,1)} %all-gather.9.cloned.1.call-done, bf16[2048,4096]{1,0:T(8,128)(2,1)} %param.11), kind=kOutput, calls=%fused_computation.55 | convolution fusion | flops 4295491584 | bytes 19922944 | tf_op jit(solution)/shard_map/dot_general | solution.py:41
  58.5 40.3 %all-gather.7.cloned.1.call-done = bf16[4096,4,128]{2,0,1:T(8,128)(2,1)} async-done(((bf16[256,4,128]{2,0,1:T(8,128)(2,1)}), bf16[4096,4,128]{2,0,1:T(8,128)(2,1)}) %all-gather.7.cloned.1.call-update) | async-done | bytes 4194320 | tf_op jit(solution)/shard_map/all_gather | solution.py:52
  98.8 4.7 copy.165
  106.7 4.9 gather_fusion.2
  111.6 38.4 %all-gather.5.cloned.1.call-done = bf16[4096,4,128]{2,1,0:T(4,128)(2,1)} async-done(((bf16[256,4,128]{2,1,0:T(4,128)(2,1)}), bf16[4096,4,128]{2,1,0:T(4,128)(2,1)}) %all-gather.5.cloned.1.call-update) | async-done | bytes 4194320 | tf_op jit(solution)/shard_map/all_gather | solution.py:51
  150.0 7.4 %gather_fusion = bf16[20,128,4,128]{3,2,1,0:T(4,128)(2,1)} fusion(bf16[32,128,4,128]{3,2,1,0:T(4,128)(2,1)} %bitcast.211, s32[1024]{0:T(1024)S(1)} %get-tuple-element.35), kind=kCustom, calls=%fused_computation | custom fusion | bytes 5242960 | tf_op jit(solution)/shard_map/gather | solution.py:65
  157.4 7.6 %gather_fusion.3 = bf16[20,128,4,128]{3,2,1,0:T(4,128)(2,1)} fusion(bf16[32,128,4,128]{3,2,1,0:T(4,128)(2,1)} %bitcast.212, s32[1024]{0:T(1024)S(1)} %get-tuple-element.34), kind=kCustom, calls=%fused_computation.3 | custom fusion | bytes 5242960 | tf_op jit(solution)/shard_map/gather | solution.py:65
  173.4 4.5 fusion.12
  177.9 4.3 fusion.15
  185.0 11.8 %fusion.38 = f32[2560,4,128]{0,2,1:T(8,128)} fusion(bf16[128,4,4,128]{0,3,2,1:T(8,128)(2,1)S(1)} %bitcast.226, f32[4,2560,128,4]{2,1,3,0:T(8,128)} %copy-done, f32[4,4,128]{2,1,0:T(4,128)S(1)} %bitcast.233, pred[128,2560]{0,1:T(8,128)(4,1)S(1)} %compare_or_fusion.1), kind=kOutput, calls=%fused_computation.53 | convolution fusion | flops 1363148800 | bytes 27074560 | tf_op jit(solution)/shard_map/gnij,ignd->jgd/dot_general | solution.py:25
  196.8 16.6 %fusion.61 = f32[128,4,4]{0,2,1:T(4,128)S(1)} fusion(bf16[2560,4,128,1]{2,0,3,1:T(8,128)(2,1)S(1)} %bitcast.221, f32[4,2560,128,4]{2,1,3,0:T(8,128)} %copy-done, f32[4,4,128]{2,1,0:T(4,128)S(1)} %bitcast.234, pred[128,2560]{0,1:T(8,128)(4,1)S(1)} %compare_or_fusion.1, bf16[128,4,4,128]{0,3,2,1:T(8,128)(2,1)S(1)} %bitcast.227), kind=kOutput, calls=%fused_computation.67 | convolution fusion | flops 8069576704 | bytes 24461312 | tf_op jit(solution)/shard_map/gnij,jgd->ignd/dot_general | solution.py:74
  213.4 15.1 %fusion.11 = bf16[4,4,128,2560]{2,3,1,0:T(8,128)(2,1)} fusion(f32[4,2560,128,4]{2,1,3,0:T(8,128)} %copy-done, f32[4,4,128]{2,1,0:T(4,128)S(1)} %bitcast.239, f32[4,4,128]{2,1,0:T(4,128)S(1)} %bitcast.235, pred[128,2560]{0,1:T(8,128)(4,1)S(1)} %compare_or_fusion.1, bf16[2560,4,128,1]{2,0,3,1:T(8,128)(2,1)S(1)} %bitcast.222, ...), kind=kOutput, calls=%fused_computation.26 | convolution fusion | flops 1378877440 | bytes 34947072 | tf_op jit(solution)/shard_map/ignd,jgd->gnij/dot_general | solution.py:26
  228.5 5.6 fusion.79
  237.0 6.3 %copy.186 = f32[2560,4,128]{2,0,1:T(8,128)} copy(f32[2560,4,128]{0,2,1:T(8,128)} %fusion.38) | data formatting | bytes 10485760 | tf_op jit(solution)/shard_map/gnij,ignd->jgd/transpose | solution.py:25
  243.4 5.5 copy.187
  259.0 11.9 %fusion.41 = f32[2560,4,128]{0,2,1:T(8,128)} fusion(bf16[128,4,4,128]{0,3,2,1:T(8,128)(2,1)S(1)} %bitcast.223, f32[4,2560,128,4]{2,1,3,0:T(8,128)} %copy-done.1, f32[4,4,128]{2,1,0:T(4,128)S(1)} %bitcast.236, pred[128,2560]{0,1:T(8,128)(4,1)S(1)} %compare_or_fusion), kind=kOutput, calls=%fused_computation.54 | convolution fusion | flops 1363148800 | bytes 27074560 | tf_op jit(solution)/shard_map/gnij,ignd->jgd/dot_general | solution.py:25
  270.8 16.8 %fusion.58 = f32[128,4,4]{0,2,1:T(4,128)S(1)} fusion(bf16[2560,4,128,1]{2,0,3,1:T(8,128)(2,1)S(1)} %bitcast.219, f32[4,2560,128,4]{2,1,3,0:T(8,128)} %copy-done.1, f32[4,4,128]{2,1,0:T(4,128)S(1)} %bitcast.237, pred[128,2560]{0,1:T(8,128)(4,1)S(1)} %compare_or_fusion, bf16[128,4,4,128]{0,3,2,1:T(8,128)(2,1)S(1)} %bitcast.224), kind=kOutput, calls=%fused_computation.66 | convolution fusion | flops 8069576704 | bytes 24461312 | tf_op jit(solution)/shard_map/gnij,jgd->ignd/dot_general | solution.py:74
  287.6 15.1 %fusion.2 = bf16[4,4,128,2560]{2,3,1,0:T(8,128)(2,1)} fusion(f32[4,2560,128,4]{2,1,3,0:T(8,128)} %copy-done.1, f32[4,4,128]{2,1,0:T(4,128)S(1)} %bitcast.240, f32[4,4,128]{2,1,0:T(4,128)S(1)} %bitcast.238, pred[128,2560]{0,1:T(8,128)(4,1)S(1)} %compare_or_fusion, bf16[2560,4,128,1]{2,0,3,1:T(8,128)(2,1)S(1)} %bitcast.220, ...), kind=kOutput, calls=%fused_computation.13 | convolution fusion | flops 1378877440 | bytes 34947072 | tf_op jit(solution)/shard_map/ignd,jgd->gnij/dot_general | solution.py:26
  302.7 5.6 fusion.80
  311.2 5.9 %copy.190 = f32[2560,4,128]{2,0,1:T(8,128)} copy(f32[2560,4,128]{0,2,1:T(8,128)} %fusion.41) | data formatting | bytes 10485760 | tf_op jit(solution)/shard_map/gnij,ignd->jgd/transpose | solution.py:25
  317.1 5.5 copy.191
  326.9 13.7 %scatter_fusion = f32[32,128,4,128]{3,1,2,0:T(8,128)} fusion(f32[32,128,4,128]{3,1,2,0:T(8,128)} %broadcast.69.clone.1, s32[20]{0:T(128)S(1)} %copy-done.13, f32[20,128,4,128]{3,1,2,0:T(8,128)} %copy.182), kind=kCustom, calls=%fused_computation.6 | custom fusion | flops 1310720 | bytes 15728720 | tf_op jit(solution)/shard_map/scatter-add | solution.py:91
  340.7 4.4 broadcast.69.clone
  345.0 13.5 %scatter_fusion.2 = f32[32,128,4,128]{3,1,2,0:T(8,128)} fusion(f32[32,128,4,128]{3,1,2,0:T(8,128)} %broadcast.69.clone, s32[20]{0:T(128)S(1)} %copy-done.13, f32[20,128,4,128]{3,1,2,0:T(8,128)} %copy.187), kind=kCustom, calls=%fused_computation.8 | custom fusion | flops 1310720 | bytes 15728720 | tf_op jit(solution)/shard_map/scatter-add | solution.py:92
  358.6 13.7 %scatter_fusion.1 = f32[32,128,4,128]{3,1,2,0:T(8,128)} fusion(f32[32,128,4,128]{3,1,2,0:T(8,128)} %scatter_fusion, s32[20]{0:T(128)S(1)} %copy-done.11, f32[20,128,4,128]{3,1,2,0:T(8,128)} %copy.183), kind=kCustom, calls=%fused_computation.7 | custom fusion | flops 1310720 | bytes 15728720 | tf_op jit(solution)/shard_map/scatter-add | solution.py:91
  372.2 13.6 %scatter_fusion.3 = f32[32,128,4,128]{3,1,2,0:T(8,128)} fusion(f32[32,128,4,128]{3,1,2,0:T(8,128)} %scatter_fusion.2, s32[20]{0:T(128)S(1)} %copy-done.11, f32[20,128,4,128]{3,1,2,0:T(8,128)} %copy.191), kind=kCustom, calls=%fused_computation.9 | custom fusion | flops 1310720 | bytes 15728720 | tf_op jit(solution)/shard_map/scatter-add | solution.py:92
  385.9 6.6 %pad_maximum_fusion = f32[32,128,4,256]{3,1,2,0:T(8,128)S(1)} fusion(f32[32,128,4,128]{3,1,2,0:T(8,128)} %scatter_fusion.3, f32[32,128,4,128]{3,1,2,0:T(8,128)} %scatter_fusion.1), kind=kLoop, calls=%fused_computation.36 | loop fusion | flops 4194304 | bytes 33554432 | tf_op jit(solution)/shard_map/concatenate | solution.py:93
  392.5 6.1 %copy.192 = f32[32,128,4,256]{3,1,0,2:T(8,128)} copy(f32[32,128,4,256]{3,1,2,0:T(8,128)S(1)} %pad_maximum_fusion) | data formatting | bytes 33554432 | tf_op jit(solution)/shard_map/concatenate | solution.py:93
  398.6 8.9 %fusion.56 = bf16[1,128,4,4,128]{4,1,3,2,0:T(8,128)(2,1)S(1)} fusion(bf16[2560,4,128,1]{2,0,3,1:T(8,128)(2,1)} %bitcast.206, bf16[4,4,128,2560]{2,3,1,0:T(8,128)(2,1)} %fusion.11), kind=kOutput, calls=%fused_computation.64 | convolution fusion | flops 1342439424 | bytes 13631488 | tf_op jit(solution)/shard_map/gnij,jgd->ignd/dot_general | solution.py:28
  407.6 9.4 %fusion.57 = bf16[1,128,4,4,128]{4,1,3,2,0:T(8,128)(2,1)S(1)} fusion(bf16[2560,4,128,1]{2,0,3,1:T(8,128)(2,1)S(1)} %bitcast.204, bf16[4,4,128,2560]{2,3,1,0:T(8,128)(2,1)} %fusion.2), kind=kOutput, calls=%fused_computation.65 | convolution fusion | flops 1342439424 | bytes 13631488 | tf_op jit(solution)/shard_map/gnij,jgd->ignd/dot_general | solution.py:28
  418.9 157.1 %reduce-scatter.2.cloned.1.call-done = f32[256,4,256]{2,0,1:T(8,128)} async-done(((f32[4096,4,256]{2,0,1:T(8,128)}), f32[256,4,256]{2,0,1:T(8,128)}) %reduce-scatter.2.cloned.1.call-update) | async-done | bytes 1048592 | tf_op jit(solution)/shard_map/reduce_scatter | solution.py:96
  (78 shorter events, 56.7 us)
Async XLA Ops:
  7.2 38.2 %all-gather.9.cloned.1.call-start = ((), (), s32[]{:S(2)}) async-start(), calls=%async_computation.3 | async-start | bytes 3145728 | tf_op jit(solution)/shard_map/all_gather | solution.py:42
  7.9 90.9 %all-gather.7.cloned.1.call-start = ((), (), s32[]{:S(2)}) async-start(), calls=%async_computation.2 | async-start | bytes 4456448 | tf_op jit(solution)/shard_map/all_gather | solution.py:52
  9.7 140.4 %all-gather.5.cloned.1.call-start = ((), (), s32[]{:S(2)}) async-start(), calls=%async_computation.1 | async-start | bytes 4456448 | tf_op jit(solution)/shard_map/all_gather | solution.py:51
  10.4 565.6 %reduce-scatter.2.cloned.1.call-start = ((), (), s32[]{:S(2)}) async-start(), calls=%async_computation.4 | async-start | bytes 17825792 | tf_op jit(solution)/shard_map/reduce_scatter | solution.py:96
  35.1 0.6 copy-start.10
  35.1 0.6 copy-start.12
  165.1 5.4 copy-start.3
  165.1 6.1 %copy-start.2 = (bf16[20,128,4,128]{3,2,1,0:T(4,128)(2,1)S(1)}, bf16[20,128,4,128]{3,2,1,0:T(4,128)(2,1)}, u32[]{:S(2)}) copy-start(bf16[20,128,4,128]{3,2,1,0:T(4,128)(2,1)} %gather_fusion) | copy-start | bytes 7864324
  165.1 8.3 %copy-start.5 = (bf16[128,16,128]{2,0,1:T(8,128)(2,1)S(1)}, bf16[128,16,128]{2,0,1:T(8,128)(2,1)}, u32[]{:S(2)}) copy-start(bf16[128,16,128]{2,0,1:T(8,128)(2,1)} %copy.163) | copy-start | bytes 1572868
  177.9 7.1 %copy-start = (f32[4,2560,128,4]{2,1,3,0:T(8,128)}, f32[4,2560,128,4]{2,1,3,0:T(8,128)S(1)}, u32[]{:S(2)}) copy-start(f32[4,2560,128,4]{2,1,3,0:T(8,128)S(1)} %get-tuple-element.33) | copy-start | bytes 62914564
  177.9 7.1 %copy-start.9 = (bf16[128,2048]{0,1:T(8,128)(2,1)S(1)}, bf16[128,2048]{0,1:T(8,128)(2,1)}, u32[]{:S(2)}) copy-start(bf16[128,2048]{0,1:T(8,128)(2,1)} %copy.216) | copy-start | bytes 1572868
  185.0 11.8 %copy-start.7 = (bf16[20,128,4,128]{3,1,0,2:T(8,128)(2,1)S(1)}, bf16[20,128,4,128]{3,1,0,2:T(8,128)(2,1)}, u32[]{:S(2)}) copy-start(bf16[20,128,4,128]{3,1,0,2:T(8,128)(2,1)} %copy.166) | copy-start | bytes 7864324
  237.0 11.8 %copy-start.4 = (bf16[128,16,128]{2,0,1:T(8,128)(2,1)S(1)}, bf16[128,16,128]{2,0,1:T(8,128)(2,1)}, u32[]{:S(2)}) copy-start(bf16[128,16,128]{2,0,1:T(8,128)(2,1)} %copy.173) | copy-start | bytes 1572868
  251.8 7.1 %copy-start.1 = (f32[4,2560,128,4]{2,1,3,0:T(8,128)}, f32[4,2560,128,4]{2,1,3,0:T(8,128)S(1)}, u32[]{:S(2)}) copy-start(f32[4,2560,128,4]{2,1,3,0:T(8,128)S(1)} %get-tuple-element.31) | copy-start | bytes 62914564
  251.8 7.1 %copy-start.8 = (bf16[128,2048]{0,1:T(8,128)(2,1)S(1)}, bf16[128,2048]{0,1:T(8,128)(2,1)}, u32[]{:S(2)}) copy-start(bf16[128,2048]{0,1:T(8,128)(2,1)} %copy.217) | copy-start | bytes 1572868
  258.9 11.9 %copy-start.6 = (bf16[20,128,4,128]{3,1,0,2:T(8,128)(2,1)S(1)}, bf16[20,128,4,128]{3,1,0,2:T(8,128)(2,1)}, u32[]{:S(2)}) copy-start(bf16[20,128,4,128]{3,1,0,2:T(8,128)(2,1)} %copy.175) | copy-start | bytes 7864324
  317.1 9.8 %copy-start.13 = (s32[20]{0:T(128)S(1)}, s32[20]{0:T(128)}, u32[]{:S(2)}) copy-start(s32[20]{0:T(128)} %copy-done.12) | copy-start | bytes 244
  340.7 17.9 %copy-start.11 = (s32[20]{0:T(128)S(1)}, s32[20]{0:T(128)}, u32[]{:S(2)}) copy-start(s32[20]{0:T(128)} %copy-done.10) | copy-start | bytes 244
Sparse Core Ops, SparseCore 0:
  9.5 35.8 all-gather.8
  48.2 50.5 all-gather.6
  100.9 49.0 all-gather.4
  398.8 177.1 reduce-scatter.1
where the time goes:
time: 596 us; the launch traced here: 586 us
  waiting for transfers between devices  239 us (40%)
  matrix products  135 us (23%)
  local copies, waits for them, and re-layouts  98 us (16%)
  other arithmetic  76.3 us (13%)
  blocking collectives  23.1 us (4%)
  between operations  14.5 us (2%)
    reduce_scatter x1, waiting for transfers between devices, on_device(): home = lax.psum_scatter(combined, 'ctx', scatter_dimension=0, tiled=True)  157 us
    all_gather x1, waiting for transfers between devices, on_device(): lax.all_gather(value, 'ctx', axis=0, tiled=True)  40.3 us
    all_gather x1, waiting for transfers between devices, on_device(): lax.all_gather(key, 'ctx', axis=0, tiled=True)  38.4 us
    dot_general x2, matrix products, on_device(): jnp.einsum('gnij,jgd->ignd', probs, v_near.astype(jnp.float32), precision...  33.4 us
    dot_general x2, matrix products, backward_pair(): jnp.einsum('ignd,jgd->gnij', do_block, v_block, preferred_element_type=jn...  30.2 us
    scatter-add x2, other arithmetic, on_device(): grad_k_all.at[listed].add(part_k.reshape(slots, BLK, kv_here, width))  27.4 us
    scatter-add x2, other arithmetic, on_device(): grad_v_all.at[listed].add(part_v.reshape(slots, BLK, kv_here, width))  27.2 us
    dot_general x2, matrix products, backward_pair(): jnp.einsum('gnij,ignd->jgd', rounded, do_block, preferred_element_type=jn...  23.7 us
  transfers between devices with their start and end apart: 4, of which 4 were waited for; matrix products, arithmetic and copies ran while one was open for 10% of the time, Pallas kernels for 0%

commit v1 on v0

--- a/solution.py
+++ b/solution.py
@@ -5,6 +5,18 @@
 from jax.sharding import PartitionSpec as P
 
 BLK = 128
+
+
+def gather_by_bits(x, axis, dim):
+    ways, here = (lax.axis_size(axis), lax.axis_index(axis))
+    grown, reach = (x, 1)
+    while reach < ways:
+        theirs = lax.ppermute(grown, axis, [(d, d ^ reach) for d in range(ways)])
+        mine_first = jnp.concatenate([grown, theirs], axis=dim)
+        theirs_first = jnp.concatenate([theirs, grown], axis=dim)
+        grown = jnp.where(here & reach == 0, mine_first, theirs_first)
+        reach = 2 * reach
+    return grown
 
 
 def score_pair(q_block, scope_q, k_block, scope_k, scale):
@@ -48,7 +60,7 @@
     do_blocks = d_out.reshape(blocks, BLK, kv_here, group, width)
     own_scope = scope_ids.reshape(blocks, BLK).astype(jnp.float32)
     all_keys, all_values, all_scope = (
-        lax.all_gather(key, "ctx", axis=0, tiled=True),
+        gather_by_bits(key, "ctx", 0),
         lax.all_gather(value, "ctx", axis=0, tiled=True),
         lax.all_gather(scope_ids.astype(jnp.bfloat16), "ctx", axis=0, tiled=True),
     )

time: 596 us -> 682 us (1.14)
  other arithmetic: 76.3 us -> 119 us
  waiting for transfers between devices: 239 us -> 277 us
    ppermute x0 -> x4, waiting for transfers between devices: none -> 120 us  [gather_by_bits(): theirs = lax.ppermute(grown, axis, [(d, d ^ reach) for d in range(ways)])]
    select_n x0 -> x4, other arithmetic: none -> 42.9 us  [gather_by_bits(): grown = jnp.where(here & reach == 0, mine_first, theirs_first)]
    all_gather x1, waiting for transfers between devices: 40.3 us -> 0.01 us  [on_device(): lax.all_gather(value, 'ctx', axis=0, tiled=True)]
    all_gather x1 -> x0, waiting for transfers between devices: 38.4 us -> none  [on_device(): lax.all_gather(key, 'ctx', axis=0, tiled=True)]
  transfers between devices with their start and end apart: 4 -> 7, of which waited for: 4 -> 4; matrix products, arithmetic and copies ran while one was open for 10% -> 31% of each run, Pallas kernels for 0% -> 0%
where the time goes in v1:
time: 682 us; the launch traced here: 673 us
  waiting for transfers between devices  277 us (41%)
  matrix products  137 us (20%)
  other arithmetic  119 us (17%)
  local copies, waits for them, and re-layouts  103 us (15%)
  blocking collectives  22.6 us (3%)
  between operations  14.3 us (2%)
    reduce_scatter x1, waiting for transfers between devices, on_device(): home = lax.psum_scatter(combined, 'ctx', scatter_dimension=0, tiled=True)  156 us
    ppermute x4, waiting for transfers between devices, gather_by_bits(): theirs = lax.ppermute(grown, axis, [(d, d ^ reach) for d in range(ways)])  120 us
    select_n x4, other arithmetic, gather_by_bits(): grown = jnp.where(here & reach == 0, mine_first, theirs_first)  42.9 us
    dot_general x2, matrix products, on_device(): jnp.einsum('gnij,jgd->ignd', probs, v_near.astype(jnp.float32), precision...  33.9 us
    dot_general x2, matrix products, backward_pair(): jnp.einsum('ignd,jgd->gnij', do_block, v_block, preferred_element_type=jn...  30.4 us
    scatter-add x2, other arithmetic, on_device(): grad_k_all.at[listed].add(part_k.reshape(slots, BLK, kv_here, width))  27.3 us
    scatter-add x2, other arithmetic, on_device(): grad_v_all.at[listed].add(part_v.reshape(slots, BLK, kv_here, width))  27.3 us
    dot_general x2, matrix products, backward_pair(): jnp.einsum('gnij,ignd->jgd', rounded, do_block, preferred_element_type=jn...  23.4 us
  transfers between devices with their start and end apart: 7, of which 4 were waited for; matrix products, arithmetic and copies ran while one was open for 31% of the time, Pallas kernels for 0%

profile of v1, /device:TPU:0, one launch (start us, length us, event | category | flops | bytes accessed | tf_op | source)
XLA Modules:
  0.0 673.5 jit_solution(8169810487055574525)
XLA Ops:
  11.8 22.6 %all-gather = bf16[16,1,256]{2,1,0:T(2,128)(2,1)S(1)} all-gather(bf16[1,1,256]{2,1,0:T(2,128)(2,1)S(1)} %reshape.255), channel_id=1, replica_groups=mesh['ctx'=16,'head'=2] {'ctx'}, dimensions={0}, use_global_device_ids=true | all-gather | bytes 8704 | tf_op jit(solution)/shard_map/all_gather | solution.py:65
  39.2 12.4 %collective-permute-done.1 = bf16[512,4,128]{2,1,0:T(4,128)(2,1)S(1)} collective-permute-done((bf16[512,4,128]{2,1,0:T(4,128)(2,1)S(1)}, bf16[512,4,128]{2,1,0:T(4,128)(2,1)S(1)}, u32[]{:S(2)}, u32[]{:S(2)}) %collective-permute-start.1) | collective-permute-done | bytes 524320 | tf_op jit(solution)/shard_map/ppermute | solution.py:14
  54.6 39.1 %collective-permute-done.2 = bf16[1024,4,128]{2,1,0:T(4,128)(2,1)S(1)} collective-permute-done((bf16[1024,4,128]{2,1,0:T(4,128)(2,1)S(1)}, bf16[1024,4,128]{2,1,0:T(4,128)(2,1)S(1)}, u32[]{:S(2)}, u32[]{:S(2)}) %collective-permute-start.2) | collective-permute-done | bytes 1048608 | tf_op jit(solution)/shard_map/ppermute | solution.py:14
  93.7 12.9 %maximum_select_fusion.1 = bf16[2048,4,128]{2,1,0:T(4,128)(2,1)S(1)} fusion(bf16[1024,4,128]{2,1,0:T(4,128)(2,1)S(1)} %collective-permute-done.2, bf16[1024,4,128]{2,1,0:T(4,128)(2,1)S(1)} %maximum_select_fusion.2, pred[]{:T(512)S(6)} %eq.35), kind=kLoop, calls=%fused_computation.57 | loop fusion | flops 3145728 | bytes 4194305 | tf_op jit(solution)/shard_map/jit(_where)/select_n | solution.py:17
  108.7 11.9 %convolution_convert_fusion = bf16[256,2048]{1,0:T(8,128)(2,1)} fusion(bf16[256,4096]{1,0:T(8,128)(2,1)} %all-gather.6.cloned.1.call-done, bf16[2048,4096]{1,0:T(8,128)(2,1)} %param.11), kind=kOutput, calls=%fused_computation.56 | convolution fusion | flops 4295491584 | bytes 19922944 | tf_op jit(solution)/shard_map/dot_general | solution.py:53
  125.8 68.4 %collective-permute-done.3 = bf16[2048,4,128]{2,1,0:T(4,128)(2,1)} collective-permute-done((bf16[2048,4,128]{2,1,0:T(4,128)(2,1)S(1)}, bf16[2048,4,128]{2,1,0:T(4,128)(2,1)}, u32[]{:S(2)}, u32[]{:S(2)}) %collective-permute-start.3) | collective-permute-done | bytes 2097184 | tf_op jit(solution)/shard_map/ppermute | solution.py:14
  194.2 27.1 %maximum_select_fusion = bf16[4096,4,128]{2,1,0:T(4,128)(2,1)} fusion(bf16[2048,4,128]{2,1,0:T(4,128)(2,1)} %collective-permute-done.3, bf16[2048,4,128]{2,1,0:T(4,128)(2,1)S(1)} %maximum_select_fusion.1, pred[]{:T(512)S(6)} %eq.34), kind=kLoop, calls=%fused_computation.55 | loop fusion | flops 6291456 | bytes 8388609 | tf_op jit(solution)/shard_map/jit(_where)/select_n | solution.py:17
  221.3 7.6 %gather_fusion.3 = bf16[20,128,4,128]{3,2,1,0:T(4,128)(2,1)} fusion(bf16[32,128,4,128]{3,2,1,0:T(4,128)(2,1)} %bitcast.207, s32[1024]{0:T(1024)S(1)} %get-tuple-element.34), kind=kCustom, calls=%fused_computation.3 | custom fusion | bytes 5242960 | tf_op jit(solution)/shard_map/gather | solution.py:77
  229.0 7.4 %gather_fusion = bf16[20,128,4,128]{3,2,1,0:T(4,128)(2,1)} fusion(bf16[32,128,4,128]{3,2,1,0:T(4,128)(2,1)} %bitcast.208, s32[1024]{0:T(1024)S(1)} %get-tuple-element.35), kind=kCustom, calls=%fused_computation | custom fusion | bytes 5242960 | tf_op jit(solution)/shard_map/gather | solution.py:77
  254.4 11.7 %fusion.41 = f32[2560,4,128]{0,2,1:T(8,128)} fusion(bf16[128,4,4,128]{0,3,2,1:T(8,128)(2,1)S(1)} %bitcast.226, f32[4,2560,128,4]{2,1,3,0:T(8,128)} %copy-done, f32[4,4,128]{2,1,0:T(4,128)S(1)} %bitcast.233, pred[128,2560]{0,1:T(8,128)(4,1)S(1)} %compare_or_fusion), kind=kOutput, calls=%fused_computation.54 | convolution fusion | flops 1363148800 | bytes 27074560 | tf_op jit(solution)/shard_map/gnij,ignd->jgd/dot_general | solution.py:37
  266.1 6.2 copy.190
  272.3 5.5 copy.191
  287.9 11.7 %fusion.38 = f32[2560,4,128]{0,2,1:T(8,128)} fusion(bf16[128,4,4,128]{0,3,2,1:T(8,128)(2,1)S(1)} %bitcast.223, f32[4,2560,128,4]{2,1,3,0:T(8,128)} %copy-done.1, f32[4,4,128]{2,1,0:T(4,128)S(1)} %bitcast.236, pred[128,2560]{0,1:T(8,128)(4,1)S(1)} %compare_or_fusion.1), kind=kOutput, calls=%fused_computation.53 | convolution fusion | flops 1363148800 | bytes 27074560 | tf_op jit(solution)/shard_map/gnij,ignd->jgd/dot_general | solution.py:37
  299.6 6.0 copy.186
  305.6 5.4 copy.187
  315.3 13.6 %scatter_fusion.2 = f32[32,128,4,128]{3,1,2,0:T(8,128)} fusion(f32[32,128,4,128]{3,1,2,0:T(8,128)} %broadcast.72.clone, s32[20]{0:T(128)S(1)} %get-tuple-element.26, f32[20,128,4,128]{3,1,2,0:T(8,128)} %copy.187), kind=kCustom, calls=%fused_computation.8 | custom fusion | flops 1310720 | bytes 15728720 | tf_op jit(solution)/shard_map/scatter-add | solution.py:104
  329.0 13.6 %scatter_fusion.3 = f32[32,128,4,128]{3,1,2,0:T(8,128)} fusion(f32[32,128,4,128]{3,1,2,0:T(8,128)} %scatter_fusion.2, s32[20]{0:T(128)S(1)} %get-tuple-element.27, f32[20,128,4,128]{3,1,2,0:T(8,128)} %copy.191), kind=kCustom, calls=%fused_computation.9 | custom fusion | flops 1310720 | bytes 15728720 | tf_op jit(solution)/shard_map/scatter-add | solution.py:104
  347.3 4.8 gather_fusion.2
  352.0 4.7 gather_fusion.5
  360.9 17.1 %fusion.58 = f32[128,4,4]{0,2,1:T(4,128)S(1)} fusion(bf16[2560,4,128,1]{2,0,3,1:T(8,128)(2,1)S(1)} %bitcast.221, f32[4,2560,128,4]{2,1,3,0:T(8,128)} %copy-done, f32[4,4,128]{2,1,0:T(4,128)S(1)} %bitcast.234, pred[128,2560]{0,1:T(8,128)(4,1)S(1)} %compare_or_fusion, bf16[128,4,4,128]{0,3,2,1:T(8,128)(2,1)S(1)} %bitcast.227), kind=kOutput, calls=%fused_computation.68 | convolution fusion | flops 8069576704 | bytes 24461312 | tf_op jit(solution)/shard_map/gnij,jgd->ignd/dot_general | solution.py:86
  378.0 15.2 %fusion.2 = bf16[4,4,128,2560]{2,3,1,0:T(8,128)(2,1)} fusion(f32[4,2560,128,4]{2,1,3,0:T(8,128)} %copy-done, f32[4,4,128]{2,1,0:T(4,128)S(1)} %bitcast.239, f32[4,4,128]{2,1,0:T(4,128)S(1)} %bitcast.235, pred[128,2560]{0,1:T(8,128)(4,1)S(1)} %compare_or_fusion, bf16[2560,4,128,1]{2,0,3,1:T(8,128)(2,1)S(1)} %bitcast.222, ...), kind=kOutput, calls=%fused_computation.13 | convolution fusion | flops 1378877440 | bytes 34947072 | tf_op jit(solution)/shard_map/ignd,jgd->gnij/dot_general | solution.py:38
  393.2 5.6 fusion.80
  401.8 16.8 %fusion.61 = f32[128,4,4]{0,2,1:T(4,128)S(1)} fusion(bf16[2560,4,128,1]{2,0,3,1:T(8,128)(2,1)S(1)} %bitcast.219, f32[4,2560,128,4]{2,1,3,0:T(8,128)} %copy-done.1, f32[4,4,128]{2,1,0:T(4,128)S(1)} %bitcast.237, pred[128,2560]{0,1:T(8,128)(4,1)S(1)} %compare_or_fusion.1, bf16[128,4,4,128]{0,3,2,1:T(8,128)(2,1)S(1)} %bitcast.224), kind=kOutput, calls=%fused_computation.69 | convolution fusion | flops 8069576704 | bytes 24461312 | tf_op jit(solution)/shard_map/gnij,jgd->ignd/dot_general | solution.py:86
  418.6 15.3 %fusion.11 = bf16[4,4,128,2560]{2,3,1,0:T(8,128)(2,1)} fusion(f32[4,2560,128,4]{2,1,3,0:T(8,128)} %copy-done.1, f32[4,4,128]{2,1,0:T(4,128)S(1)} %bitcast.240, f32[4,4,128]{2,1,0:T(4,128)S(1)} %bitcast.238, pred[128,2560]{0,1:T(8,128)(4,1)S(1)} %compare_or_fusion.1, bf16[2560,4,128,1]{2,0,3,1:T(8,128)(2,1)S(1)} %bitcast.220, ...), kind=kOutput, calls=%fused_computation.26 | convolution fusion | flops 1378877440 | bytes 34947072 | tf_op jit(solution)/shard_map/ignd,jgd->gnij/dot_general | solution.py:38
  433.9 5.6 fusion.79
  446.7 13.8 %scatter_fusion = f32[32,128,4,128]{3,1,2,0:T(8,128)} fusion(f32[32,128,4,128]{3,1,2,0:T(8,128)} %broadcast.72.clone.1, s32[20]{0:T(128)S(1)} %get-tuple-element.26, f32[20,128,4,128]{3,1,2,0:T(8,128)} %copy.182), kind=kCustom, calls=%fused_computation.6 | custom fusion | flops 1310720 | bytes 15728720 | tf_op jit(solution)/shard_map/scatter-add | solution.py:103
  460.5 13.6 %scatter_fusion.1 = f32[32,128,4,128]{3,1,2,0:T(8,128)} fusion(f32[32,128,4,128]{3,1,2,0:T(8,128)} %scatter_fusion, s32[20]{0:T(128)S(1)} %get-tuple-element.27, f32[20,128,4,128]{3,1,2,0:T(8,128)} %copy.183), kind=kCustom, calls=%fused_computation.7 | custom fusion | flops 1310720 | bytes 15728720 | tf_op jit(solution)/shard_map/scatter-add | solution.py:103
  474.1 6.6 pad_maximum_fusion
  480.7 6.2 copy.192
  486.9 9.1 %fusion.57 = bf16[1,128,4,4,128]{4,1,3,2,0:T(8,128)(2,1)S(1)} fusion(bf16[2560,4,128,1]{2,0,3,1:T(8,128)(2,1)} %bitcast.206, bf16[4,4,128,2560]{2,3,1,0:T(8,128)(2,1)} %fusion.2), kind=kOutput, calls=%fused_computation.67 | convolution fusion | flops 1342439424 | bytes 13631488 | tf_op jit(solution)/shard_map/gnij,jgd->ignd/dot_general | solution.py:40
  496.0 9.4 %fusion.56 = bf16[1,128,4,4,128]{4,1,3,2,0:T(8,128)(2,1)S(1)} fusion(bf16[2560,4,128,1]{2,0,3,1:T(8,128)(2,1)S(1)} %bitcast.204, bf16[4,4,128,2560]{2,3,1,0:T(8,128)(2,1)} %fusion.11), kind=kOutput, calls=%fused_computation.66 | convolution fusion | flops 1342439424 | bytes 13631488 | tf_op jit(solution)/shard_map/gnij,jgd->ignd/dot_general | solution.py:40
  507.3 156.2 %reduce-scatter.2.cloned.1.call-done = f32[256,4,256]{2,0,1:T(8,128)} async-done(((f32[4096,4,256]{2,0,1:T(8,128)}), f32[256,4,256]{2,0,1:T(8,128)}) %reduce-scatter.2.cloned.1.call-update) | async-done | bytes 1048592 | tf_op jit(solution)/shard_map/reduce_scatter | solution.py:108
  (81 shorter events, 76.1 us)
Async XLA Ops:
  7.2 101.6 %all-gather.6.cloned.1.call-start = ((), (), s32[]{:S(2)}) async-start(), calls=%async_computation.2 | async-start | bytes 3145728 | tf_op jit(solution)/shard_map/all_gather | solution.py:54
  7.9 334.7 %all-gather.4.cloned.1.call-start = ((), (), s32[]{:S(2)}) async-start(), calls=%async_computation.1 | async-start | bytes 4456448 | tf_op jit(solution)/shard_map/all_gather | solution.py:64
  7.9 27.7 %collective-permute-start = (bf16[256,4,128]{2,1,0:T(4,128)(2,1)}, bf16[256,4,128]{2,1,0:T(4,128)(2,1)S(1)}, u32[]{:S(2)}, u32[]{:S(2)}) collective-permute-start(bf16[256,4,128]{2,1,0:T(4,128)(2,1)} %param.8), channel_id=1, source_target_pairs={{0,2},{2,0},{4,6},{6,4},{8,10},{10,8},{12,14},{14,12},{16,18},{18,... | collective-permute-start | bytes 786440 | tf_op jit(solution)/shard_map/ppermute | solution.py:14
  10.2 653.3 %reduce-scatter.2.cloned.1.call-start = ((), (), s32[]{:S(2)}) async-start(), calls=%async_computation.3 | async-start | bytes 17825792 | tf_op jit(solution)/shard_map/reduce_scatter | solution.py:108
  35.6 71.0 %copy-start.6 = (bf16[256,16,128]{2,1,0:T(8,128)(2,1)S(1)}, bf16[256,16,128]{2,1,0:T(8,128)(2,1)}, u32[]{:S(2)}) copy-start(bf16[256,16,128]{2,1,0:T(8,128)(2,1)} %param.7) | copy-start | bytes 3145732
  37.4 14.2 %collective-permute-start.1 = (bf16[512,4,128]{2,1,0:T(4,128)(2,1)S(1)}, bf16[512,4,128]{2,1,0:T(4,128)(2,1)S(1)}, u32[]{:S(2)}, u32[]{:S(2)}) collective-permute-start(bf16[512,4,128]{2,1,0:T(4,128)(2,1)S(1)} %maximum_select_fusion.3), channel_id=1, source_target_pairs={{0,4},{2,6},{4,0},{6,2},{8,12},{10,14},{12,8},{14,10},{16,20},{18,... | collective-permute-start | bytes 1572872 | tf_op jit(solution)/shard_map/ppermute | solution.py:14
  52.7 40.9 %collective-permute-start.2 = (bf16[1024,4,128]{2,1,0:T(4,128)(2,1)S(1)}, bf16[1024,4,128]{2,1,0:T(4,128)(2,1)S(1)}, u32[]{:S(2)}, u32[]{:S(2)}) collective-permute-start(bf16[1024,4,128]{2,1,0:T(4,128)(2,1)S(1)} %maximum_select_fusion.2), channel_id=1, source_target_pairs={{0,8},{2,10},{4,12},{6,14},{8,0},{10,2},{12,4},{14,6},{16,24},{18,... | collective-permute-start | bytes 3145736 | tf_op jit(solution)/shard_map/ppermute | solution.py:14
  106.6 87.7 %collective-permute-start.3 = (bf16[2048,4,128]{2,1,0:T(4,128)(2,1)S(1)}, bf16[2048,4,128]{2,1,0:T(4,128)(2,1)}, u32[]{:S(2)}, u32[]{:S(2)}) collective-permute-start(bf16[2048,4,128]{2,1,0:T(4,128)(2,1)S(1)} %maximum_select_fusion.1), channel_id=1, source_target_pairs={{0,16},{2,18},{4,20},{6,22},{8,24},{10,26},{12,28},{14,30},{16,0},... | collective-permute-start | bytes 6291464 | tf_op jit(solution)/shard_map/ppermute | solution.py:14
  236.4 6.4 copy-start.4
  247.3 7.1 %copy-start = (f32[4,2560,128,4]{2,1,3,0:T(8,128)}, f32[4,2560,128,4]{2,1,3,0:T(8,128)S(1)}, u32[]{:S(2)}) copy-start(f32[4,2560,128,4]{2,1,3,0:T(8,128)S(1)} %get-tuple-element.31) | copy-start | bytes 62914564
  247.3 7.1 %copy-start.9 = (bf16[128,2048]{0,1:T(8,128)(2,1)S(1)}, bf16[128,2048]{0,1:T(8,128)(2,1)}, u32[]{:S(2)}) copy-start(bf16[128,2048]{0,1:T(8,128)(2,1)} %copy.217) | copy-start | bytes 1572868
  272.3 5.6 copy-start.2
  280.8 7.1 %copy-start.1 = (f32[4,2560,128,4]{2,1,3,0:T(8,128)}, f32[4,2560,128,4]{2,1,3,0:T(8,128)S(1)}, u32[]{:S(2)}) copy-start(f32[4,2560,128,4]{2,1,3,0:T(8,128)S(1)} %get-tuple-element.33) | copy-start | bytes 62914564
  280.8 7.1 %copy-start.7 = (bf16[128,2048]{0,1:T(8,128)(2,1)S(1)}, bf16[128,2048]{0,1:T(8,128)(2,1)}, u32[]{:S(2)}) copy-start(bf16[128,2048]{0,1:T(8,128)(2,1)} %copy.216) | copy-start | bytes 1572868
  356.8 4.2 copy-start.10
  378.0 15.2 %copy-start.5 = (bf16[128,16,128]{2,0,1:T(8,128)(2,1)S(1)}, bf16[128,16,128]{2,0,1:T(8,128)(2,1)}, u32[]{:S(2)}) copy-start(bf16[128,16,128]{2,0,1:T(8,128)(2,1)} %copy.173) | copy-start | bytes 1572868
  398.8 3.0 copy-start.8
  418.6 15.3 %copy-start.3 = (bf16[128,16,128]{2,0,1:T(8,128)(2,1)S(1)}, bf16[128,16,128]{2,0,1:T(8,128)(2,1)}, u32[]{:S(2)}) copy-start(bf16[128,16,128]{2,0,1:T(8,128)(2,1)} %copy.163) | copy-start | bytes 1572868
Sparse Core Ops, SparseCore 0:
  9.5 35.8 all-gather.5
  48.2 60.8 all-gather.3
  487.0 176.4 reduce-scatter.1
